TPU v7x, 32 devices: a whole 2x2x4 slice. The times are simulated.
32 devices in a mesh: energy: 4 (over z), slab: 8 (over y, x, core).
Axes of the slice: x: 2, y: 2, z: 4, core: 2. Of those that a mesh axis runs over, the one named last changes fastest.
Arguments:
- wavefunction: bfloat16 [4, 128, 64, 256], P('energy', 'slab'), may hold values from -6 to 6
- injected_modes: int32 [4, 64], P('energy'), may hold values from 0 to 255, all different within a row
- factor_blocks: float32 [4, 128, 256, 256], P('energy', 'slab'), may hold values from -1.1 to 1.1
- pivot_inverse: float32 [4, 128, 256, 256], P('energy', 'slab'), may hold values from -1 to 2.5
- mode_velocity: float32 [4, 256], P('energy'), may hold values from 0.1 to 1
- energy_weight: float32 [4], P('energy'), may hold values from 0.5 to 8
- mode_basis: bfloat16 [256, 1024], replicated, may hold values from -0.375 to 0.375
Outputs:
- sensitivity: float32 [1024, 128], P('energy', 'slab')
Inputs may be any that keep to these rules, and one draw needn't show every extreme that they name: `injected_modes`: each energy's row names 64 different modes, and every mode is named by some energy.
All inputs are finite; a program needn't handle non-finite values.
Results may differ from a plain program's by a relative error of at most 0.0003.
Values sent between devices are 32-bit elements; how exact they have to be, the bound alone decides.
A program may use at most 128 MiB of HBM per device.

v0:
```python
import functools
import jax
import jax.numpy as jnp
from jax import lax
from jax.experimental import pallas as pl
from jax.experimental.pallas import tpu as pltpu
from jax.sharding import PartitionSpec as P

F32 = jnp.float32
BF16 = jnp.bfloat16
MESH = pl.DeviceIdType.MESH


def split(x):
    hi = x.astype(BF16)
    return hi, (x - hi.astype(F32)).astype(BF16)


def dot(a, b, transposed=False):
    return lax.dot_general(
        a, b, (((1,), (1 if transposed else 0,)), ((), ())), preferred_element_type=F32
    )


def mm(a, bh, bl, transposed=False):
    ah, al = split(a)
    rows = a.shape[0]
    both = dot(jnp.concatenate([ah, al], axis=0), bh, transposed)
    return both[:rows] + both[rows:] + dot(ah, bl, transposed)


def kernel(
    n, groups,
    wave, inj, fac, piv, vel, ew, basis,
    out,
    fh, fl, qh, ql, uh, ul, th, tl, state, wt, adj, wg, off, scaled_ref,
    inc, cur, ctot, fsend, frecv, bsend, brecv, esend, erecv,
    fs, fr, bs, br, es, er,
):
    me = lax.axis_index("slab")
    mine = lax.axis_index("energy")
    slabs, cols, modes = wave.shape
    grid = basis.shape[1]
    part = grid // groups
    all_slabs = n * slabs
    small = 2.0 / (all_slabs * cols * modes * groups * 4096.0)

    barrier = pltpu.get_barrier_semaphore()

    for k in (1, n - 1):
        pl.semaphore_signal(
            barrier, inc=1, device_id=(mine, lax.rem(me + k, n)), device_id_type=MESH
        )
    for k in range(1, groups):
        peer = lax.rem(mine + k, groups)
        pl.semaphore_signal(barrier, inc=1, device_id=(peer, me), device_id_type=MESH)

    rows_at = lax.broadcasted_iota(jnp.int32, (cols, cols), 0)
    cols_at = lax.broadcasted_iota(jnp.int32, (cols, cols), 1)
    picked = jnp.sum(
        jnp.where(rows_at == cols_at, jnp.broadcast_to(inj[...].astype(F32), (cols, cols)), 0.0),
        axis=1, keepdims=True,
    )
    mode_at = lax.broadcasted_iota(jnp.int32, (cols, modes), 1).astype(F32)
    velocity = jnp.broadcast_to(vel[...], (cols, modes))
    at_injected = jnp.sum(jnp.where(mode_at == picked, velocity, 0.0), axis=1, keepdims=True)
    scaled_ref[...] = ew[...] * (1.0 / at_injected) * velocity

    eye = (
        lax.broadcasted_iota(jnp.int32, (modes, modes), 0)
        == lax.broadcasted_iota(jnp.int32, (modes, modes), 1)
    ).astype(F32)

    off[0:modes] = eye
    off[modes:] = jnp.zeros((cols, modes), F32)
    cur[...] = jnp.zeros_like(cur)

    def chain(s, carry):
        w = wave[s].astype(F32)
        sw = scaled_ref[...] * w
        sq = sw * w
        part_sum = sq[0:8]
        for i in range(1, cols // 8):
            part_sum = part_sum + sq[8 * i : 8 * i + 8]
        tile = part_sum[:, 0:128]
        for i in range(1, modes // 128):
            tile = tile + part_sum[:, 128 * i : 128 * i + 128]
        cur[...] += tile
        own = off[modes:] + sw * small
        state[s] = own
        block = jnp.concatenate([off[0:modes], own], axis=0)
        bh, bl = split(block)
        qh[s] = bh[0:modes]
        ql[s] = bl[0:modes]
        h, l = split(fac[s])
        fh[s] = h
        fl[s] = l
        total = modes + cols
        both = dot(jnp.concatenate([bh, bl], axis=0), h)
        off[...] = both[:total] + both[total:] + dot(bh, l)
        return carry

    lax.fori_loop(0, slabs, chain, 0)
    h, l = split(off[0:modes])
    th[...] = h
    tl[...] = l

    pl.semaphore_wait(barrier, groups + 1)

    to_right = pltpu.make_async_remote_copy(
        src_ref=fsend, dst_ref=frecv, send_sem=fs, recv_sem=fr,
        device_id=(mine, lax.rem(me + 1, n)), device_id_type=MESH,
    )
    to_left = pltpu.make_async_remote_copy(
        src_ref=bsend, dst_ref=brecv, send_sem=bs, recv_sem=br,
        device_id=(mine, lax.rem(me + n - 1, n)), device_id_type=MESH,
    )

    @pl.when(me == 0)
    def _():
        inc[...] = jnp.zeros_like(inc)

    @pl.when(me > 0)
    def _():
        to_right.wait_recv()
        inc[...] = frecv[0:cols]
        cur[...] += frecv[cols : cols + 8, 0:128]

    @pl.when(me < n - 1)
    def _():
        fsend[0:cols] = mm(inc[...], th[...], tl[...]) + off[modes:]
        fsend[cols : cols + 8, 0:128] = cur[...]
        fsend[cols : cols + 8, 128:] = jnp.zeros((8, modes - 128), F32)
        to_right.start()

    def weigh(s, carry):
        now = state[s] + mm(inc[...], qh[s], ql[s])
        h, l = split(piv[s])
        wt[s] = mm(now, h, l)
        return carry

    lax.fori_loop(0, slabs, weigh, 0)

    def back(i, x):
        s = slabs - 1 - i
        x = wt[s] + mm(x, fh[s], fl[s], True)
        adj[s] = x
        return x

    exit_state = lax.fori_loop(0, slabs, back, jnp.zeros((cols, modes), F32))
    bsend[0:cols] = exit_state

    @pl.when(me == n - 1)
    def _():
        ctot[...] = cur[...]
        bsend[cols : cols + 8, 0:128] = ctot[...]
        bsend[cols : cols + 8, 128:] = jnp.zeros((8, modes - 128), F32)
        to_left.start()

    @pl.when(me < n - 1)
    def _():
        off[0:modes] = eye

        def suffix(i, carry):
            s = slabs - 1 - i
            u = mm(off[0:modes], fh[s], fl[s], True)
            off[0:modes] = u
            h, l = split(u)
            uh[s] = h
            ul[s] = l
            return carry

        lax.fori_loop(0, slabs, suffix, 0)

    def waves(s, carry):
        wg[s] = dot(wave[s], basis[...])
        return carry

    lax.fori_loop(0, slabs, waves, 0)

    @pl.when(me < n - 1)
    def _():
        to_left.wait_recv()
        inc[...] = brecv[0:cols]
        ctot[...] = brecv[cols : cols + 8, 0:128]

    @pl.when(jnp.logical_and(me > 0, me < n - 1))
    def _():
        bsend[0:cols] += mm(inc[...], th[...], tl[...], True)
        bsend[cols : cols + 8, 0:128] = ctot[...]
        bsend[cols : cols + 8, 128:] = jnp.zeros((8, modes - 128), F32)
        to_left.start()

    @pl.when(me < n - 1)
    def _():
        def join(s, carry):
            adj[s] += mm(inc[...], uh[s], ul[s])
            return carry

        lax.fori_loop(0, slabs, join, 0)

    def gradient(s, carry):
        ah, al = split(adj[s])
        ag = dot(jnp.concatenate([ah, al], axis=0), basis[...])
        row = jnp.sum(wg[s] * (ag[:cols] + ag[cols:]), axis=0, keepdims=True)
        for e in range(groups):
            esend[e, pl.ds(s, 1), :] = row[:, e * part : (e + 1) * part]
        return carry

    lax.fori_loop(0, slabs, gradient, 0)
    for e in range(groups):
        esend[e, slabs : slabs + 8, 0:128] = ctot[...]
        if part > 128:
            esend[e, slabs : slabs + 8, 128:] = jnp.zeros((8, part - 128), F32)

    copies = []
    for k in range(1, groups):
        peer = lax.rem(mine + k, groups)
        copies.append(
            pltpu.make_async_remote_copy(
                src_ref=esend.at[peer], dst_ref=erecv.at[k], send_sem=es.at[k], recv_sem=er.at[k],
                device_id=(peer, me), device_id_type=MESH,
            )
        )
        copies[-1].start()
    total = esend[mine]
    for k in range(1, groups):
        copies[k - 1].wait_recv()
        total = total + erecv[k]
    current = jnp.sum(total[slabs : slabs + 8, 0:128])
    factor = (all_slabs * grid * (2.0 / small)) / current
    out[...] = total[0:slabs] * factor
    for copy in copies:
        copy.wait_send()

    @pl.when(me < n - 1)
    def _():
        to_right.wait_send()

    @pl.when(me > 0)
    def _():
        to_left.wait_send()


def local(wavefunction, injected_modes, factor_blocks, pivot_inverse, mode_velocity, energy_weight, mode_basis):
    n = lax.axis_size("slab")
    groups = lax.axis_size("energy")
    _, slabs, cols, modes = wavefunction.shape
    grid = mode_basis.shape[1]
    part = grid // groups
    vmem = pl.BlockSpec(memory_space=pltpu.VMEM)
    result = pl.pallas_call(
        functools.partial(kernel, n, groups),
        out_shape=jax.ShapeDtypeStruct((slabs, part), F32),
        in_specs=[vmem] * 7,
        out_specs=vmem,
        scratch_shapes=[
            pltpu.VMEM((slabs, modes, modes), BF16),
            pltpu.VMEM((slabs, modes, modes), BF16),
            pltpu.VMEM((slabs, modes, modes), BF16),
            pltpu.VMEM((slabs, modes, modes), BF16),
            pltpu.VMEM((slabs, modes, modes), BF16),
            pltpu.VMEM((slabs, modes, modes), BF16),
            pltpu.VMEM((modes, modes), BF16),
            pltpu.VMEM((modes, modes), BF16),
            pltpu.VMEM((slabs, cols, modes), F32),
            pltpu.VMEM((slabs, cols, modes), F32),
            pltpu.VMEM((slabs, cols, modes), F32),
            pltpu.VMEM((slabs, cols, grid), F32),
            pltpu.VMEM((modes + cols, modes), F32),
            pltpu.VMEM((cols, modes), F32),
            pltpu.VMEM((cols, modes), F32),
            pltpu.VMEM((8, 128), F32),
            pltpu.VMEM((8, 128), F32),
            pltpu.VMEM((cols + 8, modes), F32),
            pltpu.VMEM((cols + 8, modes), F32),
            pltpu.VMEM((cols + 8, modes), F32),
            pltpu.VMEM((cols + 8, modes), F32),
            pltpu.VMEM((groups, slabs + 8, part), F32),
            pltpu.VMEM((groups, slabs + 8, part), F32),
            pltpu.SemaphoreType.DMA,
            pltpu.SemaphoreType.DMA,
            pltpu.SemaphoreType.DMA,
            pltpu.SemaphoreType.DMA,
            pltpu.SemaphoreType.DMA((groups,)),
            pltpu.SemaphoreType.DMA((groups,)),
        ],
        compiler_params=pltpu.CompilerParams(
            collective_id=0, has_side_effects=True, vmem_limit_bytes=56 * 1024 * 1024
        ),
    )(
        wavefunction[0],
        injected_modes,
        factor_blocks[0],
        pivot_inverse[0],
        mode_velocity,
        energy_weight.reshape(1, 1),
        mode_basis,
    )
    return result.T


def solution(mesh):
    return jax.shard_map(
        local,
        mesh=mesh,
        in_specs=(
            P("energy", "slab", None, None),
            P("energy", None),
            P("energy", "slab", None, None),
            P("energy", "slab", None, None),
            P("energy", None),
            P("energy"),
            P(),
        ),
        out_specs=P("energy", "slab"),
        check_vma=False,
    )
```

profile of v0, /device:TPU:0, one launch (start us, length us, event | category | flops | bytes accessed | tf_op | source)
XLA Modules:
  0.0 71.3 jit_solution(9662976245098304742)
XLA Ops:
  0.7 69.4 %shard_map.73 = f32[16,256]{1,0:T(8,128)} custom-call(bf16[16,64,256]{2,1,0:T(8,128)(2,1)} %bitcast.8, s32[1,64]{1,0:T(1,128)} %inj.1, f32[16,256,256]{2,1,0:T(8,128)} %bitcast.6, f32[16,256,256]{2,1,0:T(8,128)} %bitcast.7, f32[1,256]{1,0:T(1,128)} %vel.1, f32[1,1]{1,0:T(1,128)} %bitcast.5.ew, bf16[256,1024]{1,0:T(8,128)(2,1)} %basis.1), custom_call_target="tpu_custom_call" | custom-call | tf_op jit(solution)/shard_map/pallas_call | solution.py:252
  70.0 1.3 %copy.10 = f32[256,16]{0,1:T(8,128)} copy(f32[256,16]{0,1:T(8,128)} %bitcast.9) | data formatting | bytes 32768
where the time goes:
time: 71.6 us; the launch traced here: 71.3 us
  Pallas kernels  69.4 us (97%)
  local copies, waits for them, and re-layouts  1.32 us (2%)
    pallas_call x1, Pallas kernels, local(): pl.pallas_call(functools.partial(kernel, n, groups), out_shape=jax.ShapeD...  69.4 us

commit v1 on v0

--- a/solution.py
+++ b/solution.py
@@ -34,20 +34,26 @@
     wave, inj, fac, piv, vel, ew, basis,
     out,
     fh, fl, qh, ql, uh, ul, th, tl, state, wt, adj, wg, off, scaled_ref,
-    inc, cur, ctot, fsend, frecv, bsend, brecv, esend, erecv,
-    fs, fr, bs, br, es, er,
+    inc, cur, ctot, ps, pr, osend, orecv, tsend, trecv, isend, irecv, xsend, xrecv,
+    ysend, yrecv, jsend, jrecv, esend, erecv,
+    pair_s, pair_r, os, our, ts, tr, is_, ir, xs, xr, ys, yr, js, jr, es, er,
 ):
     me = lax.axis_index("slab")
     mine = lax.axis_index("energy")
     slabs, cols, modes = wave.shape
     grid = basis.shape[1]
     part = grid // groups
+    chips = n // 2
+    chip = me // 2
+    core = lax.rem(me, 2)
+    other = me + 1 - 2 * core
+    total = modes + cols
     all_slabs = n * slabs
     small = 2.0 / (all_slabs * cols * modes * groups * 4096.0)
 
     barrier = pltpu.get_barrier_semaphore()
 
-    for k in (1, n - 1):
+    for k in range(1, n):
         pl.semaphore_signal(
             barrier, inc=1, device_id=(mine, lax.rem(me + k, n)), device_id_type=MESH
         )
@@ -95,7 +101,6 @@
         h, l = split(fac[s])
         fh[s] = h
         fl[s] = l
-        total = modes + cols
         both = dot(jnp.concatenate([bh, bl], axis=0), h)
         off[...] = both[:total] + both[total:] + dot(bh, l)
         return carry
@@ -105,33 +110,113 @@
     th[...] = h
     tl[...] = l
 
-    pl.semaphore_wait(barrier, groups + 1)
-
-    to_right = pltpu.make_async_remote_copy(
-        src_ref=fsend, dst_ref=frecv, send_sem=fs, recv_sem=fr,
-        device_id=(mine, lax.rem(me + 1, n)), device_id_type=MESH,
-    )
-    to_left = pltpu.make_async_remote_copy(
-        src_ref=bsend, dst_ref=brecv, send_sem=bs, recv_sem=br,
-        device_id=(mine, lax.rem(me + n - 1, n)), device_id_type=MESH,
-    )
-
-    @pl.when(me == 0)
-    def _():
-        inc[...] = jnp.zeros_like(inc)
-
-    @pl.when(me > 0)
-    def _():
-        to_right.wait_recv()
-        inc[...] = frecv[0:cols]
-        cur[...] += frecv[cols : cols + 8, 0:128]
-
-    @pl.when(me < n - 1)
-    def _():
-        fsend[0:cols] = mm(inc[...], th[...], tl[...]) + off[modes:]
-        fsend[cols : cols + 8, 0:128] = cur[...]
-        fsend[cols : cols + 8, 128:] = jnp.zeros((8, modes - 128), F32)
-        to_right.start()
+    pl.semaphore_wait(barrier, n + groups - 2)
+
+    def copy_to(source, target, send, receive, device):
+        return pltpu.make_async_remote_copy(
+            src_ref=source, dst_ref=target, send_sem=send, recv_sem=receive,
+            device_id=(mine, device), device_id_type=MESH,
+        )
+
+    pair = copy_to(ps, pr, pair_s, pair_r, other)
+    entry = copy_to(isend, irecv, is_, ir, other)
+    leaving = copy_to(xsend, xrecv, xs, xr, other)
+    joining = copy_to(jsend, jrecv, js, jr, other)
+
+    def offset_to(j):
+        return copy_to(osend, orecv.at[chip], os.at[j], our.at[chip], 2 * j + 1)
+
+    def transfer_to(j, k):
+        return copy_to(tsend, trecv.at[chip], ts.at[j], tr.at[chip], 2 * j + k)
+
+    def exit_to(j):
+        return copy_to(ysend, yrecv.at[chip], ys.at[j], yr.at[chip], 2 * j)
+
+    def wait_transfer(j):
+        copy_to(tsend, trecv.at[j], ts.at[j], tr.at[j], other).wait_recv()
+
+    def wait_offset(j):
+        copy_to(osend, orecv.at[j], os.at[j], our.at[j], other).wait_recv()
+
+    def wait_exit(j):
+        copy_to(ysend, yrecv.at[j], ys.at[j], yr.at[j], other).wait_recv()
+
+    def put(ref, value, tile):
+        ref[0:cols] = value
+        ref[cols : cols + 8, 0:128] = tile
+        ref[cols : cols + 8, 128:] = jnp.zeros((8, modes - 128), F32)
+
+    inner = jnp.logical_and(chip > 0, chip < chips - 1)
+
+    ps[0:total] = off[...]
+    ps[total:, 0:128] = cur[...]
+    ps[total:, 128:] = jnp.zeros((8, modes - 128), F32)
+    pair.start()
+    pair.wait_recv()
+    cur[...] += pr[total:, 0:128]
+    ctot[...] = cur[...]
+
+    @pl.when(core == 1)
+    def _():
+        whole = mm(pr[0:total], th[...], tl[...])
+        tsend[...] = whole[0:modes]
+        put(osend, whole[modes:] + off[modes:], cur[...])
+        for j in range(chips):
+            @pl.when(j > chip)
+            def _():
+                offset_to(j).start()
+
+        @pl.when(inner)
+        def _():
+            for j in range(chips):
+                @pl.when(j > chip)
+                def _():
+                    transfer_to(j, 1).start()
+
+                @pl.when(j < chip)
+                def _():
+                    transfer_to(j, 0).start()
+
+    off[0:modes] = eye
+
+    def suffix(i, carry):
+        s = slabs - 1 - i
+        u = mm(off[0:modes], fh[s], fl[s], True)
+        off[0:modes] = u
+        h, l = split(u)
+        uh[s] = h
+        ul[s] = l
+        return carry
+
+    lax.fori_loop(0, slabs, suffix, 0)
+
+    inc[...] = jnp.zeros_like(inc)
+
+    @pl.when(core == 1)
+    def _():
+        for j in range(chips - 1):
+            @pl.when(chip > j)
+            def _():
+                if j > 0:
+                    wait_transfer(j)
+                wait_offset(j)
+                if j == 0:
+                    inc[...] = orecv[j, 0:cols]
+                else:
+                    h, l = split(trecv[j])
+                    inc[...] = mm(inc[...], h, l) + orecv[j, 0:cols]
+                ctot[...] += orecv[j, cols : cols + 8, 0:128]
+
+        put(isend, inc[...], ctot[...])
+        entry.start()
+        h, l = split(pr[0:modes])
+        inc[...] = mm(inc[...], h, l) + pr[modes:total]
+
+    @pl.when(core == 0)
+    def _():
+        entry.wait_recv()
+        inc[...] = irecv[0:cols]
+        ctot[...] = irecv[cols : cols + 8, 0:128]
 
     def weigh(s, carry):
         now = state[s] + mm(inc[...], qh[s], ql[s])
@@ -148,29 +233,23 @@
         return x
 
     exit_state = lax.fori_loop(0, slabs, back, jnp.zeros((cols, modes), F32))
-    bsend[0:cols] = exit_state
-
-    @pl.when(me == n - 1)
-    def _():
-        ctot[...] = cur[...]
-        bsend[cols : cols + 8, 0:128] = ctot[...]
-        bsend[cols : cols + 8, 128:] = jnp.zeros((8, modes - 128), F32)
-        to_left.start()
-
-    @pl.when(me < n - 1)
-    def _():
-        off[0:modes] = eye
-
-        def suffix(i, carry):
-            s = slabs - 1 - i
-            u = mm(off[0:modes], fh[s], fl[s], True)
-            off[0:modes] = u
-            h, l = split(u)
-            uh[s] = h
-            ul[s] = l
-            return carry
-
-        lax.fori_loop(0, slabs, suffix, 0)
+
+    @pl.when(core == 1)
+    def _():
+        xsend[...] = exit_state
+        leaving.start()
+
+    @pl.when(core == 0)
+    def _():
+        leaving.wait_recv()
+
+        @pl.when(chip > 0)
+        def _():
+            put(ysend, exit_state + mm(xrecv[...], th[...], tl[...], True), cur[...])
+            for j in range(chips):
+                @pl.when(j < chip)
+                def _():
+                    exit_to(j).start()
 
     def waves(s, carry):
         wg[s] = dot(wave[s], basis[...])
@@ -178,26 +257,38 @@
 
     lax.fori_loop(0, slabs, waves, 0)
 
-    @pl.when(me < n - 1)
-    def _():
-        to_left.wait_recv()
-        inc[...] = brecv[0:cols]
-        ctot[...] = brecv[cols : cols + 8, 0:128]
-
-    @pl.when(jnp.logical_and(me > 0, me < n - 1))
-    def _():
-        bsend[0:cols] += mm(inc[...], th[...], tl[...], True)
-        bsend[cols : cols + 8, 0:128] = ctot[...]
-        bsend[cols : cols + 8, 128:] = jnp.zeros((8, modes - 128), F32)
-        to_left.start()
-
-    @pl.when(me < n - 1)
-    def _():
-        def join(s, carry):
-            adj[s] += mm(inc[...], uh[s], ul[s])
-            return carry
-
-        lax.fori_loop(0, slabs, join, 0)
+    @pl.when(core == 0)
+    def _():
+        inc[...] = jnp.zeros_like(inc)
+        for j in range(chips - 1, 0, -1):
+            @pl.when(chip < j)
+            def _():
+                if j < chips - 1:
+                    wait_transfer(j)
+                wait_exit(j)
+                if j == chips - 1:
+                    inc[...] = yrecv[j, 0:cols]
+                else:
+                    h, l = split(trecv[j])
+                    inc[...] = mm(inc[...], h, l, True) + yrecv[j, 0:cols]
+                ctot[...] += yrecv[j, cols : cols + 8, 0:128]
+
+        put(jsend, inc[...], ctot[...])
+        joining.start()
+        h, l = split(pr[0:modes])
+        inc[...] = mm(inc[...], h, l, True) + xrecv[...]
+
+    @pl.when(core == 1)
+    def _():
+        joining.wait_recv()
+        inc[...] = jrecv[0:cols]
+        ctot[...] = jrecv[cols : cols + 8, 0:128]
+
+    def join(s, carry):
+        adj[s] += mm(inc[...], uh[s], ul[s])
+        return carry
+
+    lax.fori_loop(0, slabs, join, 0)
 
     def gradient(s, carry):
         ah, al = split(adj[s])
@@ -223,23 +314,45 @@
             )
         )
         copies[-1].start()
-    total = esend[mine]
+    summed = esend[mine]
     for k in range(1, groups):
         copies[k - 1].wait_recv()
-        total = total + erecv[k]
-    current = jnp.sum(total[slabs : slabs + 8, 0:128])
+        summed = summed + erecv[k]
+    current = jnp.sum(summed[slabs : slabs + 8, 0:128])
     factor = (all_slabs * grid * (2.0 / small)) / current
-    out[...] = total[0:slabs] * factor
+    out[...] = summed[0:slabs] * factor
     for copy in copies:
         copy.wait_send()
 
-    @pl.when(me < n - 1)
-    def _():
-        to_right.wait_send()
-
-    @pl.when(me > 0)
-    def _():
-        to_left.wait_send()
+    pair.wait_send()
+
+    @pl.when(core == 1)
+    def _():
+        entry.wait_send()
+        leaving.wait_send()
+        for j in range(chips):
+            @pl.when(j > chip)
+            def _():
+                offset_to(j).wait_send()
+
+        @pl.when(inner)
+        def _():
+            for j in range(chips):
+                @pl.when(j > chip)
+                def _():
+                    transfer_to(j, 1).wait_send()
+
+                @pl.when(j < chip)
+                def _():
+                    transfer_to(j, 0).wait_send()
+
+    @pl.when(core == 0)
+    def _():
+        joining.wait_send()
+        for j in range(chips):
+            @pl.when(j < chip)
+            def _():
+                exit_to(j).wait_send()
 
 
 def local(wavefunction, injected_modes, factor_blocks, pivot_inverse, mode_velocity, energy_weight, mode_basis):
@@ -272,14 +385,34 @@
             pltpu.VMEM((cols, modes), F32),
             pltpu.VMEM((8, 128), F32),
             pltpu.VMEM((8, 128), F32),
-            pltpu.VMEM((cols + 8, modes), F32),
-            pltpu.VMEM((cols + 8, modes), F32),
+            pltpu.VMEM((modes + cols + 8, modes), F32),
+            pltpu.VMEM((modes + cols + 8, modes), F32),
+            pltpu.VMEM((cols + 8, modes), F32),
+            pltpu.VMEM((n // 2, cols + 8, modes), F32),
+            pltpu.VMEM((modes, modes), F32),
+            pltpu.VMEM((n // 2, modes, modes), F32),
+            pltpu.VMEM((cols + 8, modes), F32),
+            pltpu.VMEM((cols + 8, modes), F32),
+            pltpu.VMEM((cols, modes), F32),
+            pltpu.VMEM((cols, modes), F32),
+            pltpu.VMEM((cols + 8, modes), F32),
+            pltpu.VMEM((n // 2, cols + 8, modes), F32),
             pltpu.VMEM((cols + 8, modes), F32),
             pltpu.VMEM((cols + 8, modes), F32),
             pltpu.VMEM((groups, slabs + 8, part), F32),
             pltpu.VMEM((groups, slabs + 8, part), F32),
             pltpu.SemaphoreType.DMA,
             pltpu.SemaphoreType.DMA,
+            pltpu.SemaphoreType.DMA((n // 2,)),
+            pltpu.SemaphoreType.DMA((n // 2,)),
+            pltpu.SemaphoreType.DMA((n // 2,)),
+            pltpu.SemaphoreType.DMA((n // 2,)),
+            pltpu.SemaphoreType.DMA,
+            pltpu.SemaphoreType.DMA,
+            pltpu.SemaphoreType.DMA,
+            pltpu.SemaphoreType.DMA,
+            pltpu.SemaphoreType.DMA((n // 2,)),
+            pltpu.SemaphoreType.DMA((n // 2,)),
             pltpu.SemaphoreType.DMA,
             pltpu.SemaphoreType.DMA,
             pltpu.SemaphoreType.DMA((groups,)),

time: 71.6 us -> 53.1 us (0.74)
  Pallas kernels: 69.4 us -> 50.9 us
    pallas_call x1, Pallas kernels: 69.4 us -> 50.9 us  [local(): pl.pallas_call(functools.partial(kernel, n, groups), out_shape=jax.ShapeD...]
where the time goes in v1:
time: 53.1 us; the launch traced here: 52.9 us
  Pallas kernels  50.9 us (96%)
  local copies, waits for them, and re-layouts  1.32 us (2%)
  between operations  0.66 us (1%)
    pallas_call x1, Pallas kernels, local(): pl.pallas_call(functools.partial(kernel, n, groups), out_shape=jax.ShapeD...  50.9 us
    unnamed x1, local copies, waits for them, and re-layouts  1.32 us

profile of v1, /device:TPU:0, one launch (start us, length us, event | category | flops | bytes accessed | tf_op | source)
XLA Modules:
  0.0 52.9 jit_solution(15735244607429113426)
XLA Ops:
  0.7 50.9 %shard_map.73 = f32[16,256]{1,0:T(8,128)} custom-call(bf16[16,64,256]{2,1,0:T(8,128)(2,1)} %bitcast.8, s32[1,64]{1,0:T(1,128)} %inj.1, f32[16,256,256]{2,1,0:T(8,128)} %bitcast.6, f32[16,256,256]{2,1,0:T(8,128)} %bitcast.7, f32[1,256]{1,0:T(1,128)} %vel.1, f32[1,1]{1,0:T(1,128)} %bitcast.5.ew, bf16[256,1024]{1,0:T(8,128)(2,1)} %basis.1), custom_call_target="tpu_custom_call" | custom-call | tf_op jit(solution)/shard_map/pallas_call | solution.py:365
  51.6 1.3 %copy.10 = f32[256,16]{0,1:T(8,128)} copy(f32[256,16]{0,1:T(8,128)} %bitcast.9) | data formatting | bytes 32768

commit v2 on v1

--- a/solution.py
+++ b/solution.py
@@ -31,8 +31,9 @@
 
 def kernel(
     n, groups,
-    wave, inj, fac, piv, vel, ew, basis,
+    wave, inj, fac_hbm, piv_hbm, vel, ew, basis,
     out,
+    fac, piv, ahl, fac_sem, piv_sem,
     fh, fl, qh, ql, uh, ul, th, tl, state, wt, adj, wg, off, scaled_ref,
     inc, cur, ctot, ps, pr, osend, orecv, tsend, trecv, isend, irecv, xsend, xrecv,
     ysend, yrecv, jsend, jrecv, esend, erecv,
@@ -51,6 +52,14 @@
     all_slabs = n * slabs
     small = 2.0 / (all_slabs * cols * modes * groups * 4096.0)
 
+    def factor_in(s):
+        return pltpu.make_async_copy(fac_hbm.at[s], fac.at[s], fac_sem.at[s])
+
+    for s in range(slabs):
+        factor_in(s).start()
+    pivots_in = pltpu.make_async_copy(piv_hbm, piv, piv_sem)
+    pivots_in.start()
+
     barrier = pltpu.get_barrier_semaphore()
 
     for k in range(1, n):
@@ -98,6 +107,7 @@
         bh, bl = split(block)
         qh[s] = bh[0:modes]
         ql[s] = bl[0:modes]
+        factor_in(s).wait()
         h, l = split(fac[s])
         fh[s] = h
         fl[s] = l
@@ -218,21 +228,16 @@
         inc[...] = irecv[0:cols]
         ctot[...] = irecv[cols : cols + 8, 0:128]
 
-    def weigh(s, carry):
+    pivots_in.wait()
+
+    def weigh(s, leaves):
         now = state[s] + mm(inc[...], qh[s], ql[s])
         h, l = split(piv[s])
-        wt[s] = mm(now, h, l)
-        return carry
-
-    lax.fori_loop(0, slabs, weigh, 0)
-
-    def back(i, x):
-        s = slabs - 1 - i
-        x = wt[s] + mm(x, fh[s], fl[s], True)
-        adj[s] = x
-        return x
-
-    exit_state = lax.fori_loop(0, slabs, back, jnp.zeros((cols, modes), F32))
+        weighted = mm(now, h, l)
+        wt[s] = weighted
+        return leaves + mm(weighted, qh[s], ql[s], True)
+
+    exit_state = lax.fori_loop(0, slabs, weigh, jnp.zeros((cols, modes), F32), unroll=4)
 
     @pl.when(core == 1)
     def _():
@@ -251,11 +256,19 @@
                 def _():
                     exit_to(j).start()
 
-    def waves(s, carry):
-        wg[s] = dot(wave[s], basis[...])
+    def back(i, x):
+        s = slabs - 1 - i
+        x = wt[s] + mm(x, fh[s], fl[s], True)
+        adj[s] = x
+        return x
+
+    lax.fori_loop(0, slabs, back, jnp.zeros((cols, modes), F32))
+
+    def waves(b, carry):
+        wg[b] = dot(wave[pl.ds(4 * b, 4)].reshape(4 * cols, modes), basis[...])
         return carry
 
-    lax.fori_loop(0, slabs, waves, 0)
+    lax.fori_loop(0, slabs // 4, waves, 0)
 
     @pl.when(core == 0)
     def _():
@@ -284,37 +297,41 @@
         inc[...] = jrecv[0:cols]
         ctot[...] = jrecv[cols : cols + 8, 0:128]
 
-    def join(s, carry):
-        adj[s] += mm(inc[...], uh[s], ul[s])
+    def join(b, carry):
+        for i in range(4):
+            s = 4 * b + i
+            h, l = split(adj[s] + mm(inc[...], uh[s], ul[s]))
+            ahl[b, cols * i : cols * (i + 1)] = h
+            ahl[b, cols * (4 + i) : cols * (5 + i)] = l
         return carry
 
-    lax.fori_loop(0, slabs, join, 0)
-
-    def gradient(s, carry):
-        ah, al = split(adj[s])
-        ag = dot(jnp.concatenate([ah, al], axis=0), basis[...])
-        row = jnp.sum(wg[s] * (ag[:cols] + ag[cols:]), axis=0, keepdims=True)
-        for e in range(groups):
-            esend[e, pl.ds(s, 1), :] = row[:, e * part : (e + 1) * part]
-        return carry
-
-    lax.fori_loop(0, slabs, gradient, 0)
-    for e in range(groups):
-        esend[e, slabs : slabs + 8, 0:128] = ctot[...]
+    lax.fori_loop(0, slabs // 4, join, 0)
+
+    copies = []
+    for k in list(range(1, groups)) + [0]:
+        peer = lax.rem(mine + k, groups)
+        columns = pl.ds(pl.multiple_of(peer * part, 128), part)
+        points = basis[:, columns]
+        for b in range(slabs // 4):
+            ag = dot(ahl[b], points)
+            both = wg[b, :, columns] * (ag[: 4 * cols] + ag[4 * cols :])
+            for i in range(4):
+                esend[k, 4 * b + i : 4 * b + i + 1] = jnp.sum(
+                    both[cols * i : cols * (i + 1)], axis=0, keepdims=True
+                )
+        esend[k, slabs : slabs + 8, 0:128] = ctot[...]
         if part > 128:
-            esend[e, slabs : slabs + 8, 128:] = jnp.zeros((8, part - 128), F32)
-
-    copies = []
-    for k in range(1, groups):
-        peer = lax.rem(mine + k, groups)
-        copies.append(
-            pltpu.make_async_remote_copy(
-                src_ref=esend.at[peer], dst_ref=erecv.at[k], send_sem=es.at[k], recv_sem=er.at[k],
-                device_id=(peer, me), device_id_type=MESH,
+            esend[k, slabs : slabs + 8, 128:] = jnp.zeros((8, part - 128), F32)
+        if k > 0:
+            copies.append(
+                pltpu.make_async_remote_copy(
+                    src_ref=esend.at[k], dst_ref=erecv.at[k],
+                    send_sem=es.at[k], recv_sem=er.at[k],
+                    device_id=(peer, me), device_id_type=MESH,
+                )
             )
-        )
-        copies[-1].start()
-    summed = esend[mine]
+            copies[-1].start()
+    summed = esend[0]
     for k in range(1, groups):
         copies[k - 1].wait_recv()
         summed = summed + erecv[k]
@@ -362,12 +379,18 @@
     grid = mode_basis.shape[1]
     part = grid // groups
     vmem = pl.BlockSpec(memory_space=pltpu.VMEM)
+    hbm = pl.BlockSpec(memory_space=pl.ANY)
     result = pl.pallas_call(
         functools.partial(kernel, n, groups),
         out_shape=jax.ShapeDtypeStruct((slabs, part), F32),
-        in_specs=[vmem] * 7,
+        in_specs=[vmem, vmem, hbm, hbm, vmem, vmem, vmem],
         out_specs=vmem,
         scratch_shapes=[
+            pltpu.VMEM((slabs, modes, modes), F32),
+            pltpu.VMEM((slabs, modes, modes), F32),
+            pltpu.VMEM((slabs // 4, 8 * cols, modes), BF16),
+            pltpu.SemaphoreType.DMA((slabs,)),
+            pltpu.SemaphoreType.DMA,
             pltpu.VMEM((slabs, modes, modes), BF16),
             pltpu.VMEM((slabs, modes, modes), BF16),
             pltpu.VMEM((slabs, modes, modes), BF16),
@@ -379,7 +402,7 @@
             pltpu.VMEM((slabs, cols, modes), F32),
             pltpu.VMEM((slabs, cols, modes), F32),
             pltpu.VMEM((slabs, cols, modes), F32),
-            pltpu.VMEM((slabs, cols, grid), F32),
+            pltpu.VMEM((slabs // 4, 4 * cols, grid), F32),
             pltpu.VMEM((modes + cols, modes), F32),
             pltpu.VMEM((cols, modes), F32),
             pltpu.VMEM((cols, modes), F32),
@@ -419,7 +442,7 @@
             pltpu.SemaphoreType.DMA((groups,)),
         ],
         compiler_params=pltpu.CompilerParams(
-            collective_id=0, has_side_effects=True, vmem_limit_bytes=56 * 1024 * 1024
+            collective_id=0, has_side_effects=True, vmem_limit_bytes=60 * 1024 * 1024
         ),
     )(
         wavefunction[0],

time: 53.1 us -> 43 us (0.81)
  Pallas kernels: 50.9 us -> 40.6 us
    pallas_call x1, Pallas kernels: 50.9 us -> 40.6 us  [local(): pl.pallas_call(functools.partial(kernel, n, groups), out_shape=jax.ShapeD...]
where the time goes in v2:
time: 43 us; the launch traced here: 42.6 us
  Pallas kernels  40.6 us (94%)
  local copies, waits for them, and re-layouts  1.32 us (3%)
  between operations  0.66 us (2%)
    pallas_call x1, Pallas kernels, local(): pl.pallas_call(functools.partial(kernel, n, groups), out_shape=jax.ShapeD...  40.6 us
    unnamed x1, local copies, waits for them, and re-layouts  1.32 us

profile of v2, /device:TPU:0, one launch (start us, length us, event | category | flops | bytes accessed | tf_op | source)
XLA Modules:
  0.0 42.6 jit_solution(10255309015526559203)
XLA Ops:
  0.7 40.6 %shard_map.73 = f32[16,256]{1,0:T(8,128)} custom-call(bf16[16,64,256]{2,1,0:T(8,128)(2,1)} %bitcast.8, s32[1,64]{1,0:T(1,128)} %inj.1, f32[16,256,256]{2,1,0:T(8,128)} %bitcast.6, f32[16,256,256]{2,1,0:T(8,128)} %bitcast.7, f32[1,256]{1,0:T(1,128)} %vel.1, f32[1,1]{1,0:T(1,128)} %bitcast.5.ew, bf16[256,1024]{1,0:T(8,128)(2,1)} %basis.1), custom_call_target="tpu_custom_call" | custom-call | tf_op jit(solution)/shard_map/pallas_call | solution.py:383
  41.3 1.3 %copy.10 = f32[256,16]{0,1:T(8,128)} copy(f32[256,16]{0,1:T(8,128)} %bitcast.9) | data formatting | bytes 32768

commit v3 on v2

--- a/solution.py
+++ b/solution.py
@@ -115,7 +115,7 @@
         off[...] = both[:total] + both[total:] + dot(bh, l)
         return carry
 
-    lax.fori_loop(0, slabs, chain, 0)
+    lax.fori_loop(0, slabs, chain, 0, unroll=4)
     h, l = split(off[0:modes])
     th[...] = h
     tl[...] = l
@@ -182,10 +182,6 @@
                 @pl.when(j > chip)
                 def _():
                     transfer_to(j, 1).start()
-
-                @pl.when(j < chip)
-                def _():
-                    transfer_to(j, 0).start()
 
     off[0:modes] = eye
 
@@ -198,7 +194,14 @@
         ul[s] = l
         return carry
 
-    lax.fori_loop(0, slabs, suffix, 0)
+    lax.fori_loop(0, slabs, suffix, 0, unroll=4)
+
+    @pl.when(jnp.logical_and(core == 1, inner))
+    def _():
+        for j in range(chips):
+            @pl.when(j < chip)
+            def _():
+                transfer_to(j, 0).start()
 
     inc[...] = jnp.zeros_like(inc)
 
@@ -262,7 +265,7 @@
         adj[s] = x
         return x
 
-    lax.fori_loop(0, slabs, back, jnp.zeros((cols, modes), F32))
+    lax.fori_loop(0, slabs, back, jnp.zeros((cols, modes), F32), unroll=4)
 
     def waves(b, carry):
         wg[b] = dot(wave[pl.ds(4 * b, 4)].reshape(4 * cols, modes), basis[...])
@@ -305,7 +308,7 @@
             ahl[b, cols * (4 + i) : cols * (5 + i)] = l
         return carry
 
-    lax.fori_loop(0, slabs // 4, join, 0)
+    lax.fori_loop(0, slabs // 4, join, 0, unroll=2)
 
     copies = []
     for k in list(range(1, groups)) + [0]:

time: 43 us -> 41.1 us (0.956)
  Pallas kernels: 40.6 us -> 38.7 us
    pallas_call x1, Pallas kernels: 40.6 us -> 38.7 us  [local(): pl.pallas_call(functools.partial(kernel, n, groups), out_shape=jax.ShapeD...]
where the time goes in v3:
time: 41.1 us; the launch traced here: 40.6 us
  Pallas kernels  38.7 us (94%)
  local copies, waits for them, and re-layouts  1.32 us (3%)
  between operations  0.66 us (2%)
    pallas_call x1, Pallas kernels, local(): pl.pallas_call(functools.partial(kernel, n, groups), out_shape=jax.ShapeD...  38.7 us
    unnamed x1, local copies, waits for them, and re-layouts  1.32 us

profile of v3, /device:TPU:0, one launch (start us, length us, event | category | flops | bytes accessed | tf_op | source)
XLA Modules:
  0.0 40.6 jit_solution(6351833436765077206)
XLA Ops:
  0.7 38.7 %shard_map.73 = f32[16,256]{1,0:T(8,128)} custom-call(bf16[16,64,256]{2,1,0:T(8,128)(2,1)} %bitcast.8, s32[1,64]{1,0:T(1,128)} %inj.1, f32[16,256,256]{2,1,0:T(8,128)} %bitcast.6, f32[16,256,256]{2,1,0:T(8,128)} %bitcast.7, f32[1,256]{1,0:T(1,128)} %vel.1, f32[1,1]{1,0:T(1,128)} %bitcast.5.ew, bf16[256,1024]{1,0:T(8,128)(2,1)} %basis.1), custom_call_target="tpu_custom_call" | custom-call | tf_op jit(solution)/shard_map/pallas_call | solution.py:386
  39.3 1.3 %copy.10 = f32[256,16]{0,1:T(8,128)} copy(f32[256,16]{0,1:T(8,128)} %bitcast.9) | data formatting | bytes 32768

commit v4 on v3

--- a/solution.py
+++ b/solution.py
@@ -33,7 +33,7 @@
     n, groups,
     wave, inj, fac_hbm, piv_hbm, vel, ew, basis,
     out,
-    fac, piv, ahl, fac_sem, piv_sem,
+    fac, piv, ahl, fac_sem, piv_sem, tah, tal, whole_off, incb,
     fh, fl, qh, ql, uh, ul, th, tl, state, wt, adj, wg, off, scaled_ref,
     inc, cur, ctot, ps, pr, osend, orecv, tsend, trecv, isend, irecv, xsend, xrecv,
     ysend, yrecv, jsend, jrecv, esend, erecv,
@@ -49,14 +49,16 @@
     core = lax.rem(me, 2)
     other = me + 1 - 2 * core
     total = modes + cols
+    half = slabs // 2
     all_slabs = n * slabs
     small = 2.0 / (all_slabs * cols * modes * groups * 4096.0)
 
     def factor_in(s):
         return pltpu.make_async_copy(fac_hbm.at[s], fac.at[s], fac_sem.at[s])
 
-    for s in range(slabs):
+    for s in range(half):
         factor_in(s).start()
+        factor_in(half + s).start()
     pivots_in = pltpu.make_async_copy(piv_hbm, piv, piv_sem)
     pivots_in.start()
 
@@ -86,39 +88,55 @@
         == lax.broadcasted_iota(jnp.int32, (modes, modes), 1)
     ).astype(F32)
 
-    off[0:modes] = eye
-    off[modes:] = jnp.zeros((cols, modes), F32)
+    for k in range(2):
+        off[k, 0:modes] = eye
+        off[k, modes:] = jnp.zeros((cols, modes), F32)
     cur[...] = jnp.zeros_like(cur)
 
-    def chain(s, carry):
-        w = wave[s].astype(F32)
-        sw = scaled_ref[...] * w
-        sq = sw * w
-        part_sum = sq[0:8]
-        for i in range(1, cols // 8):
-            part_sum = part_sum + sq[8 * i : 8 * i + 8]
-        tile = part_sum[:, 0:128]
-        for i in range(1, modes // 128):
-            tile = tile + part_sum[:, 128 * i : 128 * i + 128]
-        cur[...] += tile
-        own = off[modes:] + sw * small
-        state[s] = own
-        block = jnp.concatenate([off[0:modes], own], axis=0)
-        bh, bl = split(block)
-        qh[s] = bh[0:modes]
-        ql[s] = bl[0:modes]
-        factor_in(s).wait()
-        h, l = split(fac[s])
-        fh[s] = h
-        fl[s] = l
-        both = dot(jnp.concatenate([bh, bl], axis=0), h)
-        off[...] = both[:total] + both[total:] + dot(bh, l)
+    def chain(t, carry):
+        blocks = []
+        for k in range(2):
+            s = k * half + t
+            w = wave[s].astype(F32)
+            sw = scaled_ref[...] * w
+            sq = sw * w
+            part_sum = sq[0:8]
+            for i in range(1, cols // 8):
+                part_sum = part_sum + sq[8 * i : 8 * i + 8]
+            tile = part_sum[:, 0:128]
+            for i in range(1, modes // 128):
+                tile = tile + part_sum[:, 128 * i : 128 * i + 128]
+            cur[...] += tile
+            own = off[k, modes:] + sw * small
+            state[s] = own
+            bh, bl = split(jnp.concatenate([off[k, 0:modes], own], axis=0))
+            qh[s] = bh[0:modes]
+            ql[s] = bl[0:modes]
+            factor_in(s).wait()
+            h, l = split(fac[s])
+            fh[s] = h
+            fl[s] = l
+            blocks.append((bh, bl, h, l))
+        results = []
+        for bh, bl, h, l in blocks:
+            both = dot(jnp.concatenate([bh, bl], axis=0), h)
+            results.append(both[:total] + both[total:] + dot(bh, l))
+        for k in range(2):
+            off[k] = results[k]
         return carry
 
-    lax.fori_loop(0, slabs, chain, 0, unroll=4)
-    h, l = split(off[0:modes])
+    lax.fori_loop(0, half, chain, 0, unroll=2)
+    h, l = split(off[0, 0:modes])
+    tah[...] = h
+    tal[...] = l
+    h, l = split(off[1, 0:modes])
+    joined = mm(off[0], h, l)
+    h, l = split(joined[0:modes])
     th[...] = h
     tl[...] = l
+    whole_off[...] = joined[modes:] + off[1, modes:]
+    ps[0:modes] = joined[0:modes]
+    ps[modes:total] = whole_off[...]
 
     pl.semaphore_wait(barrier, n + groups - 2)
 
@@ -158,7 +176,6 @@
 
     inner = jnp.logical_and(chip > 0, chip < chips - 1)
 
-    ps[0:total] = off[...]
     ps[total:, 0:128] = cur[...]
     ps[total:, 128:] = jnp.zeros((8, modes - 128), F32)
     pair.start()
@@ -170,7 +187,7 @@
     def _():
         whole = mm(pr[0:total], th[...], tl[...])
         tsend[...] = whole[0:modes]
-        put(osend, whole[modes:] + off[modes:], cur[...])
+        put(osend, whole[modes:] + whole_off[...], cur[...])
         for j in range(chips):
             @pl.when(j > chip)
             def _():
@@ -183,18 +200,23 @@
                 def _():
                     transfer_to(j, 1).start()
 
-    off[0:modes] = eye
+    for k in range(2):
+        off[k, 0:modes] = eye
 
     def suffix(i, carry):
-        s = slabs - 1 - i
-        u = mm(off[0:modes], fh[s], fl[s], True)
-        off[0:modes] = u
-        h, l = split(u)
-        uh[s] = h
-        ul[s] = l
+        results = []
+        for k in range(2):
+            s = k * half + half - 1 - i
+            results.append(mm(off[k, 0:modes], fh[s], fl[s], True))
+        for k in range(2):
+            s = k * half + half - 1 - i
+            off[k, 0:modes] = results[k]
+            h, l = split(results[k])
+            uh[s] = h
+            ul[s] = l
         return carry
 
-    lax.fori_loop(0, slabs, suffix, 0, unroll=4)
+    lax.fori_loop(0, half, suffix, 0, unroll=2)
 
     @pl.when(jnp.logical_and(core == 1, inner))
     def _():
@@ -233,14 +255,22 @@
 
     pivots_in.wait()
 
-    def weigh(s, leaves):
-        now = state[s] + mm(inc[...], qh[s], ql[s])
-        h, l = split(piv[s])
-        weighted = mm(now, h, l)
-        wt[s] = weighted
-        return leaves + mm(weighted, qh[s], ql[s], True)
-
-    exit_state = lax.fori_loop(0, slabs, weigh, jnp.zeros((cols, modes), F32), unroll=4)
+    incb[...] = mm(inc[...], tah[...], tal[...]) + off[0, modes:]
+
+    def weigh(t, leaves):
+        left = []
+        for k, entering in enumerate((inc, incb)):
+            s = k * half + t
+            now = state[s] + mm(entering[...], qh[s], ql[s])
+            h, l = split(piv[s])
+            weighted = mm(now, h, l)
+            wt[s] = weighted
+            left.append(leaves[k] + mm(weighted, qh[s], ql[s], True))
+        return tuple(left)
+
+    nothing = jnp.zeros((cols, modes), F32)
+    leaves = lax.fori_loop(0, half, weigh, (nothing, nothing), unroll=2)
+    exit_state = leaves[0] + mm(leaves[1], tah[...], tal[...], True)
 
     @pl.when(core == 1)
     def _():
@@ -259,13 +289,16 @@
                 def _():
                     exit_to(j).start()
 
-    def back(i, x):
-        s = slabs - 1 - i
-        x = wt[s] + mm(x, fh[s], fl[s], True)
-        adj[s] = x
-        return x
-
-    lax.fori_loop(0, slabs, back, jnp.zeros((cols, modes), F32), unroll=4)
+    def back(i, held):
+        left = []
+        for k in range(2):
+            s = k * half + half - 1 - i
+            x = wt[s] + mm(held[k], fh[s], fl[s], True)
+            adj[s] = x
+            left.append(x)
+        return tuple(left)
+
+    lax.fori_loop(0, half, back, (nothing, nothing), unroll=2)
 
     def waves(b, carry):
         wg[b] = dot(wave[pl.ds(4 * b, 4)].reshape(4 * cols, modes), basis[...])
@@ -300,15 +333,15 @@
         inc[...] = jrecv[0:cols]
         ctot[...] = jrecv[cols : cols + 8, 0:128]
 
-    def join(b, carry):
+    incb[...] = adj[half] + mm(inc[...], uh[half], ul[half])
+
+    for b in range(slabs // 4):
         for i in range(4):
             s = 4 * b + i
-            h, l = split(adj[s] + mm(inc[...], uh[s], ul[s]))
+            entering = incb if s < half else inc
+            h, l = split(adj[s] + mm(entering[...], uh[s], ul[s]))
             ahl[b, cols * i : cols * (i + 1)] = h
             ahl[b, cols * (4 + i) : cols * (5 + i)] = l
-        return carry
-
-    lax.fori_loop(0, slabs // 4, join, 0, unroll=2)
 
     copies = []
     for k in list(range(1, groups)) + [0]:
@@ -394,6 +427,10 @@
             pltpu.VMEM((slabs // 4, 8 * cols, modes), BF16),
             pltpu.SemaphoreType.DMA((slabs,)),
             pltpu.SemaphoreType.DMA,
+            pltpu.VMEM((modes, modes), BF16),
+            pltpu.VMEM((modes, modes), BF16),
+            pltpu.VMEM((cols, modes), F32),
+            pltpu.VMEM((cols, modes), F32),
             pltpu.VMEM((slabs, modes, modes), BF16),
             pltpu.VMEM((slabs, modes, modes), BF16),
             pltpu.VMEM((slabs, modes, modes), BF16),
@@ -406,7 +443,7 @@
             pltpu.VMEM((slabs, cols, modes), F32),
             pltpu.VMEM((slabs, cols, modes), F32),
             pltpu.VMEM((slabs // 4, 4 * cols, grid), F32),
-            pltpu.VMEM((modes + cols, modes), F32),
+            pltpu.VMEM((2, modes + cols, modes), F32),
             pltpu.VMEM((cols, modes), F32),
             pltpu.VMEM((cols, modes), F32),
             pltpu.VMEM((8, 128), F32),

time: 41.1 us -> 39.4 us (0.959)
  Pallas kernels: 38.7 us -> 37 us
    pallas_call x1, Pallas kernels: 38.7 us -> 37 us  [local(): pl.pallas_call(functools.partial(kernel, n, groups), out_shape=jax.ShapeD...]
where the time goes in v4:
time: 39.4 us; the launch traced here: 39 us
  Pallas kernels  37 us (94%)
  local copies, waits for them, and re-layouts  1.32 us (3%)
  between operations  0.66 us (2%)
    pallas_call x1, Pallas kernels, local(): pl.pallas_call(functools.partial(kernel, n, groups), out_shape=jax.ShapeD...  37 us
    unnamed x1, local copies, waits for them, and re-layouts  1.32 us

profile of v4, /device:TPU:0, one launch (start us, length us, event | category | flops | bytes accessed | tf_op | source)
XLA Modules:
  0.0 39.0 jit_solution(15580745780709056119)
XLA Ops:
  0.7 37.0 %shard_map.73 = f32[16,256]{1,0:T(8,128)} custom-call(bf16[16,64,256]{2,1,0:T(8,128)(2,1)} %bitcast.8, s32[1,64]{1,0:T(1,128)} %inj.1, f32[16,256,256]{2,1,0:T(8,128)} %bitcast.6, f32[16,256,256]{2,1,0:T(8,128)} %bitcast.7, f32[1,256]{1,0:T(1,128)} %vel.1, f32[1,1]{1,0:T(1,128)} %bitcast.5.ew, bf16[256,1024]{1,0:T(8,128)(2,1)} %basis.1), custom_call_target="tpu_custom_call" | custom-call | tf_op jit(solution)/shard_map/pallas_call | solution.py:419
  37.7 1.3 %copy.10 = f32[256,16]{0,1:T(8,128)} copy(f32[256,16]{0,1:T(8,128)} %bitcast.9) | data formatting | bytes 32768

commit v5 on v4

--- a/solution.py
+++ b/solution.py
@@ -225,6 +225,12 @@
             def _():
                 transfer_to(j, 0).start()
 
+    def waves(b, carry):
+        wg[b] = dot(wave[pl.ds(4 * b, 4)].reshape(4 * cols, modes), basis[...])
+        return carry
+
+    lax.fori_loop(0, slabs // 4, waves, 0)
+
     inc[...] = jnp.zeros_like(inc)
 
     @pl.when(core == 1)
@@ -299,12 +305,6 @@
         return tuple(left)
 
     lax.fori_loop(0, half, back, (nothing, nothing), unroll=2)
-
-    def waves(b, carry):
-        wg[b] = dot(wave[pl.ds(4 * b, 4)].reshape(4 * cols, modes), basis[...])
-        return carry
-
-    lax.fori_loop(0, slabs // 4, waves, 0)
 
     @pl.when(core == 0)
     def _():

time: 39.4 us -> 39.4 us (level)
  no operation moved by 1% of the time
where the time goes in v5:
time: 39.4 us; the launch traced here: 39 us
  Pallas kernels  37 us (94%)
  local copies, waits for them, and re-layouts  1.32 us (3%)
  between operations  0.66 us (2%)
    pallas_call x1, Pallas kernels, local(): pl.pallas_call(functools.partial(kernel, n, groups), out_shape=jax.ShapeD...  37 us
    unnamed x1, local copies, waits for them, and re-layouts  1.32 us

profile of v5, /device:TPU:0, one launch (start us, length us, event | category | flops | bytes accessed | tf_op | source)
XLA Modules:
  0.0 39.0 jit_solution(5808830220406177091)
XLA Ops:
  0.7 37.0 %shard_map.73 = f32[16,256]{1,0:T(8,128)} custom-call(bf16[16,64,256]{2,1,0:T(8,128)(2,1)} %bitcast.8, s32[1,64]{1,0:T(1,128)} %inj.1, f32[16,256,256]{2,1,0:T(8,128)} %bitcast.6, f32[16,256,256]{2,1,0:T(8,128)} %bitcast.7, f32[1,256]{1,0:T(1,128)} %vel.1, f32[1,1]{1,0:T(1,128)} %bitcast.5.ew, bf16[256,1024]{1,0:T(8,128)(2,1)} %basis.1), custom_call_target="tpu_custom_call" | custom-call | tf_op jit(solution)/shard_map/pallas_call | solution.py:419
  37.7 1.3 %copy.10 = f32[256,16]{0,1:T(8,128)} copy(f32[256,16]{0,1:T(8,128)} %bitcast.9) | data formatting | bytes 32768
